TPU v7x, 32 devices: a whole 2x2x4 slice. The times are simulated.
32 devices in a mesh: group: 2 (over x), blk: 16 (over z, y, core).
Axes of the slice: x: 2, y: 2, z: 4, core: 2. Of those that a mesh axis runs over, the one named last changes fastest.
Arguments:
- queries: bfloat16 [4096, 512], P(('group', 'blk')), parts along dimension 0, may hold values from -8 to 8
- keys: bfloat16 [4096, 512], P(('group', 'blk')), parts along dimension 0, may hold values from -8 to 8
- values: bfloat16 [4096, 512], P(('group', 'blk')), parts along dimension 0, may hold values from -6 to 6
- outputs: bfloat16 [4096, 512], P(('group', 'blk')), parts along dimension 0, may hold values from -6 to 6
- grad_out: bfloat16 [4096, 512], P(('group', 'blk')), parts along dimension 0, may hold values from -16 to 16
- block_mask: int32 [32, 16], P(('group', 'blk')), parts along dimension 0, may hold values from 0 to 1, as said below
- neighbours: int32 [4096, 6], P(('group', 'blk')), parts along dimension 0, may hold values from -1 to 2047, as said below
- conv_weight: float32 [6, 512], replicated, may hold values from -0.125 to 0.125
Outputs:
- grad_queries: bfloat16 [4096, 512], P(('group', 'blk')), parts along dimension 0
- grad_keys: bfloat16 [4096, 512], P(('group', 'blk')), parts along dimension 0
- grad_values: bfloat16 [4096, 512], P(('group', 'blk')), parts along dimension 0
There are 2 independent parts, one for each index of `group`. A program takes and returns all parts, laid end to end along the dimension named above; an argument that names none is the same for every part. Nothing has to cross between parts.
Inputs may be any that keep to these rules, and one draw needn't show every extreme that they name: Every diagonal entry is 1; block_mask[a, b] = 1 where the 128 queries of block a (one index of blk) attend to the keys of block b. `neighbours`: each entry is -1 or a token index that differs from its row's own index by at most 128; the difference 128 occurs.
All inputs are finite; a program needn't handle non-finite values.
Results may differ from a plain program's by a relative error of at most 0.0052.
Values may be sent and summed in bfloat16 or wider, within the bound.
A program may use at most 128 MiB of HBM per device.

v0:
```python
import math

import jax
import jax.numpy as jnp
from jax import lax
from jax.sharding import PartitionSpec as P

HEADS = 8
HD = 64


NEG_LARGE = -1e30


def shifted(array, axis, by):
    length = lax.axis_size(axis)
    pairs = [(i, i + by) for i in range(length) if 0 <= i + by < length]
    return lax.ppermute(array, axis, pairs)


def blockwise(portions, running, step_fn, row_count):
    row_total = portions[0].shape[0]
    group_size = math.gcd(row_total // row_count, max(1, 512 // row_count))
    block_rows = group_size * row_count
    step_count = row_total // block_rows
    stacked = tuple(
        (
            array_part.reshape((step_count, block_rows) + array_part.shape[1:])
            for array_part in portions
        )
    )

    def advance(current, inputs):
        return (step_fn(current, inputs[1:], inputs[0] * block_rows), None)

    running, ignored = lax.scan(
        advance, running, (jnp.arange(step_count, dtype=jnp.int32),) + stacked
    )
    return running


def body(queries, keys, values, outputs, grad_out, block_mask, neighbours, conv_weight):
    row_count = queries.shape[0]
    channels = queries.shape[1]
    block_total = block_mask.shape[1]
    score_scale = HD ** (-0.5)
    highest = lax.Precision.HIGHEST
    own_index = lax.axis_index("blk")
    first_row = own_index * row_count
    query_heads = queries.reshape(row_count, HEADS, HD)
    grad_heads = grad_out.reshape(row_count, HEADS, HD)
    row_delta = jnp.einsum(
        "thd,thd->th",
        grad_heads,
        outputs.reshape(row_count, HEADS, HD),
        preferred_element_type=jnp.float32,
    )
    block_ids = jnp.arange(block_total, dtype=jnp.int32)
    mask_line = block_mask[0] > 0

    def live_keys(begin_row, block_rows):
        owners = (begin_row + jnp.arange(block_rows, dtype=jnp.int32)) // row_count
        return jnp.any((owners[:, None] == block_ids[None, :]) & mask_line[None, :], axis=1)

    def key_scores(key_block, live_cols):
        block_rows = key_block.shape[0]
        scores = score_scale * jnp.einsum(
            "thd,shd->ths",
            query_heads,
            key_block.reshape(block_rows, HEADS, HD),
            preferred_element_type=jnp.float32,
        )
        return jnp.where(live_cols[None, None, :], scores, NEG_LARGE)

    def query_terms(value_block, key_block, weights):
        block_rows = value_block.shape[0]
        grad_prob = jnp.einsum(
            "thd,shd->ths",
            grad_heads,
            value_block.reshape(block_rows, HEADS, HD),
            preferred_element_type=jnp.float32,
        )
        grad_score = weights * (grad_prob - row_delta[:, :, None])
        key_wide = key_block.reshape(block_rows, HEADS, HD).astype(jnp.float32)
        return score_scale * jnp.einsum("ths,shd->thd", grad_score, key_wide, precision=highest)

    empty_heads = jnp.zeros((row_count, HEADS, HD), jnp.float32)
    start_max = jnp.full((row_count, HEADS), NEG_LARGE, jnp.float32)
    start_sum = jnp.zeros((row_count, HEADS), jnp.float32)

    def total_step(running, blocks, begin_row):
        live_cols = live_keys(begin_row, blocks[0].shape[0])

        def total_compute_block(current):
            running_max, normalizer = current
            scores = key_scores(blocks[0], live_cols)
            new_max = jnp.maximum(running_max, jnp.max(scores, axis=2))
            weights = jnp.where(
                live_cols[None, None, :], jnp.exp(scores - new_max[:, :, None]), 0.0
            )
            return (new_max, normalizer * jnp.exp(running_max - new_max) + jnp.sum(weights, axis=2))

        return lax.cond(jnp.any(live_cols), total_compute_block, lambda current: current, running)

    running_max, normalizer = blockwise(
        (lax.all_gather(keys, "blk", axis=0, tiled=True),),
        (start_max, start_sum),
        total_step,
        row_count,
    )
    log_total = running_max + jnp.log(normalizer)

    def query_step(running, blocks, begin_row):
        live_cols = live_keys(begin_row, blocks[0].shape[0])

        def query_compute_block(current):
            scores = key_scores(blocks[0], live_cols)
            weights = jnp.where(
                live_cols[None, None, :], jnp.exp(scores - log_total[:, :, None]), 0.0
            )
            return current + query_terms(blocks[1], blocks[0], weights)

        return lax.cond(jnp.any(live_cols), query_compute_block, lambda current: current, running)

    grad_query_sum = blockwise(
        (
            lax.all_gather(keys, "blk", axis=0, tiled=True),
            lax.all_gather(values, "blk", axis=0, tiled=True),
        ),
        empty_heads,
        query_step,
        row_count,
    )
    grad_queries = grad_query_sum.reshape(row_count, channels).astype(jnp.bfloat16)
    all_log, all_delta, all_mask = (
        lax.all_gather(log_total, "blk", axis=0, tiled=True),
        lax.all_gather(row_delta, "blk", axis=0, tiled=True),
        lax.all_gather(block_mask, "blk", axis=0, tiled=True),
    )
    own_column = jnp.sum(jnp.where(block_ids[None, :] == own_index, all_mask, 0), axis=1) > 0
    key_heads = keys.reshape(row_count, HEADS, HD)
    value_heads = values.reshape(row_count, HEADS, HD)

    def owner_step(running, blocks, begin_row):
        block_rows = blocks[0].shape[0]
        owners = (begin_row + jnp.arange(block_rows, dtype=jnp.int32)) // row_count
        live_rows = jnp.any((owners[:, None] == block_ids[None, :]) & own_column[None, :], axis=1)

        def owner_compute_block(current):
            grad_key_sum, grad_value_sum = current
            visit_queries = blocks[0].reshape(block_rows, HEADS, HD)
            visit_grads = blocks[1].reshape(block_rows, HEADS, HD)
            visit_log = lax.dynamic_slice_in_dim(all_log, begin_row, block_rows, 0)
            visit_delta = lax.dynamic_slice_in_dim(all_delta, begin_row, block_rows, 0)
            scores = score_scale * jnp.einsum(
                "shd,thd->sht", visit_queries, key_heads, preferred_element_type=jnp.float32
            )
            weights = jnp.where(
                live_rows[:, None, None], jnp.exp(scores - visit_log[:, :, None]), 0.0
            )
            grad_prob = jnp.einsum(
                "shd,thd->sht", visit_grads, value_heads, preferred_element_type=jnp.float32
            )
            grad_score = weights * (grad_prob - visit_delta[:, :, None])
            weights_low = weights.astype(jnp.bfloat16)
            score_low = grad_score.astype(jnp.bfloat16)
            grad_value_sum = grad_value_sum + jnp.einsum(
                "sht,shd->thd", weights_low, visit_grads, preferred_element_type=jnp.float32
            )
            grad_key_sum = grad_key_sum + score_scale * jnp.einsum(
                "sht,shd->thd", score_low, visit_queries, preferred_element_type=jnp.float32
            )
            return (grad_key_sum, grad_value_sum)

        return lax.cond(jnp.any(live_rows), owner_compute_block, lambda current: current, running)

    grad_key_sum, grad_value_sum = blockwise(
        (
            lax.all_gather(queries, "blk", axis=0, tiled=True),
            lax.all_gather(grad_out, "blk", axis=0, tiled=True),
        ),
        (empty_heads, empty_heads),
        owner_step,
        row_count,
    )
    usable = neighbours >= 0
    targets = jnp.where(usable, neighbours - first_row + row_count, 0)
    contributions = jnp.where(
        usable[:, :, None], conv_weight[None, :, :] * grad_out.astype(jnp.float32)[:, None, :], 0.0
    )
    spread = (
        jnp.zeros((3 * row_count, channels), jnp.float32)
        .at[targets.reshape(-1)]
        .add(contributions.reshape(-1, channels))
    )
    from_above = shifted(spread[:row_count].astype(jnp.bfloat16), "blk", -1).astype(jnp.float32)
    from_below = shifted(spread[2 * row_count :].astype(jnp.bfloat16), "blk", 1).astype(jnp.float32)
    conv_grad = spread[row_count : 2 * row_count] + from_above + from_below
    grad_keys = grad_key_sum.reshape(row_count, channels).astype(jnp.bfloat16)
    grad_values = (grad_value_sum.reshape(row_count, channels) + conv_grad).astype(jnp.bfloat16)
    return (grad_queries, grad_keys, grad_values)


def solution(mesh):
    return jax.shard_map(
        body,
        mesh=mesh,
        in_specs=(
            P(("group", "blk"), None),
            P(("group", "blk"), None),
            P(("group", "blk"), None),
            P(("group", "blk"), None),
            P(("group", "blk"), None),
            P(("group", "blk"), None),
            P(("group", "blk"), None),
            P(),
        ),
        out_specs=(P(("group", "blk"), None), P(("group", "blk"), None), P(("group", "blk"), None)),
        check_vma=False,
    )
```

profile of v0, /device:TPU:0, one launch (start us, length us, event | category | flops | bytes accessed | tf_op | source)
XLA Modules:
  0.0 288.0 jit_solution(17951514051960827256)
XLA Ops:
  14.7 9.4 %scatter_custom_fusion = f32[384,512]{1,0:T(8,128)S(1)} fusion(s32[768]{0:T(1024)S(1)} %fusion.71, f32[768,512]{1,0:T(8,128)} %mul.100, f32[]{:T(128)} %constant.229.clone.1, pred[768]{0:T(1024)(128)(4,1)S(1)} %broadcast_in_dim.131), kind=kCustom, calls=%fused_computation.89 | custom fusion | flops 786432 | bytes 2361344 | tf_op jit(solution)/shard_map/scatter-add | solution.py:194
  31.2 24.4 %all-gather = s32[16,1,16]{2,1,0:T(1,128)S(1)} all-gather(s32[1,1,16]{2,1,0:T(1,128)S(1)} %bitcast.133), channel_id=1, replica_groups=mesh['group'=2,'blk'=16] {'blk'}, dimensions={0}, use_global_device_ids=true | all-gather | bytes 1088 | tf_op jit(solution)/shard_map/all_gather | solution.py:138
  55.6 19.0 %all_gather.28 = f32[2048,8]{0,1:T(8,128)} all-gather(f32[128,8]{0,1:T(8,128)S(1)} %fusion.70), channel_id=1, replica_groups=mesh['group'=2,'blk'=16] {'blk'}, dimensions={0}, use_global_device_ids=true | all-gather | bytes 69632 | tf_op jit(solution)/shard_map/all_gather | solution.py:137
  78.1 18.7 %all-gather.8.cloned.1.call-done = bf16[2048,512]{1,0:T(8,128)(2,1)} async-done(((bf16[128,512]{1,0:T(8,128)(2,1)}), bf16[2048,512]{1,0:T(8,128)(2,1)}) %all-gather.8.cloned.1.call-update) | async-done | bytes 2097168 | tf_op jit(solution)/shard_map/all_gather | solution.py:128
  96.7 4.1 %copy.55 = bf16[4,512,512]{1,2,0:T(8,128)(2,1)} copy(bf16[4,512,512]{2,1,0:T(8,128)(2,1)} %bitcast.127) | data formatting | bytes 4194304
  100.9 38.2 %all-gather.10.cloned.1.call-done = bf16[2048,512]{1,0:T(8,128)(2,1)} async-done(((bf16[128,512]{1,0:T(8,128)(2,1)}), bf16[2048,512]{1,0:T(8,128)(2,1)}) %all-gather.10.cloned.1.call-update) | async-done | bytes 2097168 | tf_op jit(solution)/shard_map/all_gather | solution.py:179
  139.1 4.1 %copy.58 = bf16[4,512,512]{1,2,0:T(8,128)(2,1)} copy(bf16[4,512,512]{2,1,0:T(8,128)(2,1)} %bitcast.128) | data formatting | bytes 4194304
  143.2 16.5 %while.46 = (s32[]{:T(128)}, f32[128,8]{0,1:T(8,128)S(1)}, f32[128,8]{0,1:T(8,128)S(1)}, s32[4]{0:T(128)S(1)}, pred[16]{0:T(512)(128)(4,1)S(1)}, /*index=5*/bf16...) while((s32[]{:T(128)}, f32[128,8]{0,1:T(8,128)S(1)}, ...), condition=%wide.region_7.8_spmd.clone, body=%wide.region_0.7_spmd.clone.sunk | while | flops 71345664 | bytes 5973748 | solution.py:36
  159.8 21.1 %all_gather.26 = f32[2048,8]{0,1:T(8,128)} all-gather(f32[128,8]{0,1:T(8,128)S(1)} %log_add_fusion), channel_id=1, replica_groups=mesh['group'=2,'blk'=16] {'blk'}, dimensions={0}, use_global_device_ids=true | all-gather | bytes 69632 | tf_op jit(solution)/shard_map/all_gather | solution.py:136
  181.4 4.2 %copy.59 = bf16[4,512,512]{1,2,0:T(8,128)(2,1)} copy(bf16[4,512,512]{2,1,0:T(8,128)(2,1)} %bitcast.125) | data formatting | bytes 4194304
  186.9 48.9 %while.48 = (s32[]{:T(128)}, f32[128,8,64]{0,2,1:T(8,128)}, f32[128,8,64]{0,2,1:T(8,128)S(1)}, s32[4]{0:T(128)}, pred[16]{0:T(512)(128)(4,1)}, /*index=5*/bf16[4...) while((s32[]{:T(128)}, f32[128,8,64]{0,2,1:T(8,128)}, ...), condition=%wide.region_20.21_spmd.clone, body=%wide.region_15.20_spmd.clone.sunk | while | flops 272342528 | bytes 11916642 | solution.py:36
  190.7 8.4 %conditional.11 = ((f32[128,8,64]{0,2,1:T(8,128)}, f32[128,8,64]{0,2,1:T(8,128)S(1)})) conditional(s32[]{:T(128)} %convert_element_type.85, (f32[128,8,64]{0,2,1:T(8,128)}, f32[128,8,64]{0,2,1:T(8,128)S(1)}) %tuple.158, (pred[512,16]{0,1:T(8,128)(4,1)S(1)}, bf16[4,512,512]{1,2,0:T(8,128)(2,1)}, s32[]{:T(128)}, bf16[128,8,64]{0,2,1:T(8,128)(2,1)}, ...), branch_computations={%region_17.17_spmd, %region_18.19_spmd} | conditional | flops 272309760 | bytes 11904067 | solution.py:175
  203.0 8.4 %conditional.11 = ((f32[128,8,64]{0,2,1:T(8,128)}, f32[128,8,64]{0,2,1:T(8,128)S(1)})) conditional(s32[]{:T(128)} %convert_element_type.85, (f32[128,8,64]{0,2,1:T(8,128)}, f32[128,8,64]{0,2,1:T(8,128)S(1)}) %tuple.158, (pred[512,16]{0,1:T(8,128)(4,1)S(1)}, bf16[4,512,512]{1,2,0:T(8,128)(2,1)}, s32[]{:T(128)}, bf16[128,8,64]{0,2,1:T(8,128)(2,1)}, ...), branch_computations={%region_17.17_spmd, %region_18.19_spmd} | conditional | flops 272309760 | bytes 11904067 | solution.py:175
  215.2 8.4 %conditional.11 = ((f32[128,8,64]{0,2,1:T(8,128)}, f32[128,8,64]{0,2,1:T(8,128)S(1)})) conditional(s32[]{:T(128)} %convert_element_type.85, (f32[128,8,64]{0,2,1:T(8,128)}, f32[128,8,64]{0,2,1:T(8,128)S(1)}) %tuple.158, (pred[512,16]{0,1:T(8,128)(4,1)S(1)}, bf16[4,512,512]{1,2,0:T(8,128)(2,1)}, s32[]{:T(128)}, bf16[128,8,64]{0,2,1:T(8,128)(2,1)}, ...), branch_computations={%region_17.17_spmd, %region_18.19_spmd} | conditional | flops 272309760 | bytes 11904067 | solution.py:175
  227.4 8.3 %conditional.11 = ((f32[128,8,64]{0,2,1:T(8,128)}, f32[128,8,64]{0,2,1:T(8,128)S(1)})) conditional(s32[]{:T(128)} %convert_element_type.85, (f32[128,8,64]{0,2,1:T(8,128)}, f32[128,8,64]{0,2,1:T(8,128)S(1)}) %tuple.158, (pred[512,16]{0,1:T(8,128)(4,1)S(1)}, bf16[4,512,512]{1,2,0:T(8,128)(2,1)}, s32[]{:T(128)}, bf16[128,8,64]{0,2,1:T(8,128)(2,1)}, ...), branch_computations={%region_17.17_spmd, %region_18.19_spmd} | conditional | flops 272309760 | bytes 11904067 | solution.py:175
  235.8 41.2 %while.47 = (s32[]{:T(128)}, f32[128,8,64]{0,2,1:T(8,128)S(1)}, s32[4]{0:T(128)S(1)}, pred[16]{0:T(512)(128)(4,1)}, bf16[4,512,512]{1,2,0:T(8,128)(2,1)}, /*inde...) while((s32[]{:T(128)}, f32[128,8,64]{0,2,1:T(8,128)S(1)}, ...), condition=%wide.region_13.14_spmd.clone, body=%wide.region_8.13_spmd.clone.sunk | while | flops 540188160 | bytes 13432152 | solution.py:36
  239.1 7.0 %conditional.10 = (f32[128,8,64]{0,2,1:T(8,128)S(1)}) conditional(s32[]{:T(128)} %convert_element_type.84, f32[128,8,64]{0,2,1:T(8,128)S(1)} %get-tuple-element.1115, (pred[512,16]{0,1:T(8,128)(4,1)S(1)}, bf16[4,512,512]{1,2,0:T(8,128)(2,1)}, s32[]{:T(128)}, bf16[128,8,64]{0,2,1:T(8,128)(2,1)S(1)}, f32[128,8]{0,1:T(8,128)}, ...), branch_computations={%region_10.10_spmd, %region_11.12_spmd} | conditional | flops 540155392 | bytes 13419617 | solution.py:123
  242.8 3.3 %fusion.23 = f32[128,8,64]{0,2,1:T(8,128)S(1)} fusion(f32[128,8,64]{0,2,1:T(8,128)S(1)} %get-tuple-element.578, bf16[512,8,64]{0,2,1:T(8,128)(2,1)S(1)} %bitcast.116, f32[8,512,128]{2,1,0:T(8,128)S(1)} %fusion.74, f32[8,512,128]{2,1,0:T(8,128)} %fusion.73, f32[128,8]{0,1:T(8,128)S(1)} %copy-done.11, f32[128,8]{0,1:T(8,128)S(1)} %copy-done.13, ...), kind=kOutput, calls=%fused_computation.22 | convolution fusion | flops 405929984 | bytes 5251584 | tf_op jit(solution)/shard_map/while/body/eval_jaxpr/cond/branch_1_fun/ths,shd->thd/dot_general | solution.py:85
  249.4 7.0 %conditional.10 = (f32[128,8,64]{0,2,1:T(8,128)S(1)}) conditional(s32[]{:T(128)} %convert_element_type.84, f32[128,8,64]{0,2,1:T(8,128)S(1)} %get-tuple-element.1115, (pred[512,16]{0,1:T(8,128)(4,1)S(1)}, bf16[4,512,512]{1,2,0:T(8,128)(2,1)}, s32[]{:T(128)}, bf16[128,8,64]{0,2,1:T(8,128)(2,1)S(1)}, f32[128,8]{0,1:T(8,128)}, ...), branch_computations={%region_10.10_spmd, %region_11.12_spmd} | conditional | flops 540155392 | bytes 13419617 | solution.py:123
  253.1 3.3 %fusion.23 = f32[128,8,64]{0,2,1:T(8,128)S(1)} fusion(f32[128,8,64]{0,2,1:T(8,128)S(1)} %get-tuple-element.578, bf16[512,8,64]{0,2,1:T(8,128)(2,1)S(1)} %bitcast.116, f32[8,512,128]{2,1,0:T(8,128)S(1)} %fusion.74, f32[8,512,128]{2,1,0:T(8,128)} %fusion.73, f32[128,8]{0,1:T(8,128)S(1)} %copy-done.11, f32[128,8]{0,1:T(8,128)S(1)} %copy-done.13, ...), kind=kOutput, calls=%fused_computation.22 | convolution fusion | flops 405929984 | bytes 5251584 | tf_op jit(solution)/shard_map/while/body/eval_jaxpr/cond/branch_1_fun/ths,shd->thd/dot_general | solution.py:85
  259.7 7.0 %conditional.10 = (f32[128,8,64]{0,2,1:T(8,128)S(1)}) conditional(s32[]{:T(128)} %convert_element_type.84, f32[128,8,64]{0,2,1:T(8,128)S(1)} %get-tuple-element.1115, (pred[512,16]{0,1:T(8,128)(4,1)S(1)}, bf16[4,512,512]{1,2,0:T(8,128)(2,1)}, s32[]{:T(128)}, bf16[128,8,64]{0,2,1:T(8,128)(2,1)S(1)}, f32[128,8]{0,1:T(8,128)}, ...), branch_computations={%region_10.10_spmd, %region_11.12_spmd} | conditional | flops 540155392 | bytes 13419617 | solution.py:123
  263.5 3.3 %fusion.23 = f32[128,8,64]{0,2,1:T(8,128)S(1)} fusion(f32[128,8,64]{0,2,1:T(8,128)S(1)} %get-tuple-element.578, bf16[512,8,64]{0,2,1:T(8,128)(2,1)S(1)} %bitcast.116, f32[8,512,128]{2,1,0:T(8,128)S(1)} %fusion.74, f32[8,512,128]{2,1,0:T(8,128)} %fusion.73, f32[128,8]{0,1:T(8,128)S(1)} %copy-done.11, f32[128,8]{0,1:T(8,128)S(1)} %copy-done.13, ...), kind=kOutput, calls=%fused_computation.22 | convolution fusion | flops 405929984 | bytes 5251584 | tf_op jit(solution)/shard_map/while/body/eval_jaxpr/cond/branch_1_fun/ths,shd->thd/dot_general | solution.py:85
  270.0 7.0 %conditional.10 = (f32[128,8,64]{0,2,1:T(8,128)S(1)}) conditional(s32[]{:T(128)} %convert_element_type.84, f32[128,8,64]{0,2,1:T(8,128)S(1)} %get-tuple-element.1115, (pred[512,16]{0,1:T(8,128)(4,1)S(1)}, bf16[4,512,512]{1,2,0:T(8,128)(2,1)}, s32[]{:T(128)}, bf16[128,8,64]{0,2,1:T(8,128)(2,1)S(1)}, f32[128,8]{0,1:T(8,128)}, ...), branch_computations={%region_10.10_spmd, %region_11.12_spmd} | conditional | flops 540155392 | bytes 13419617 | solution.py:123
  273.8 3.3 %fusion.23 = f32[128,8,64]{0,2,1:T(8,128)S(1)} fusion(f32[128,8,64]{0,2,1:T(8,128)S(1)} %get-tuple-element.578, bf16[512,8,64]{0,2,1:T(8,128)(2,1)S(1)} %bitcast.116, f32[8,512,128]{2,1,0:T(8,128)S(1)} %fusion.74, f32[8,512,128]{2,1,0:T(8,128)} %fusion.73, f32[128,8]{0,1:T(8,128)S(1)} %copy-done.11, f32[128,8]{0,1:T(8,128)S(1)} %copy-done.13, ...), kind=kOutput, calls=%fused_computation.22 | convolution fusion | flops 405929984 | bytes 5251584 | tf_op jit(solution)/shard_map/while/body/eval_jaxpr/cond/branch_1_fun/ths,shd->thd/dot_general | solution.py:85
  (210 shorter events, 106.8 us)
Async XLA Ops:
  7.2 68.1 %all-gather.6.cloned.1.call-start = ((), (), s32[]{:S(2)}) async-start(), calls=%async_computation | async-start | bytes 2228224 | tf_op jit(solution)/shard_map/all_gather | solution.py:127
  7.9 88.8 %all-gather.8.cloned.1.call-start = ((), (), s32[]{:S(2)}) async-start(), calls=%async_computation.1 | async-start | bytes 2228224 | tf_op jit(solution)/shard_map/all_gather | solution.py:128
  8.6 130.4 %all-gather.10.cloned.1.call-start = ((), (), s32[]{:S(2)}) async-start(), calls=%async_computation.2 | async-start | bytes 2228224 | tf_op jit(solution)/shard_map/all_gather | solution.py:179
  9.4 172.0 %all-gather.12.cloned.1.call-start = ((), (), s32[]{:S(2)}) async-start(), calls=%async_computation.3 | async-start | bytes 2228224 | tf_op jit(solution)/shard_map/all_gather | solution.py:180
  14.3 14.9 %copy-start.7 = (bf16[128,512]{1,0:T(8,128)(2,1)S(1)}, bf16[128,512]{1,0:T(8,128)(2,1)}, u32[]{:S(2)}) copy-start(bf16[128,512]{1,0:T(8,128)(2,1)} %param.20) | copy-start | bytes 393220
  14.6 14.8 %copy-start.4 = (bf16[128,512]{1,0:T(8,128)(2,1)S(1)}, bf16[128,512]{1,0:T(8,128)(2,1)}, u32[]{:S(2)}) copy-start(bf16[128,512]{1,0:T(8,128)(2,1)} %param.24) | copy-start | bytes 393220
  14.6 14.9 %copy-start.5 = (bf16[128,512]{1,0:T(8,128)(2,1)S(1)}, bf16[128,512]{1,0:T(8,128)(2,1)}, u32[]{:S(2)}) copy-start(bf16[128,512]{1,0:T(8,128)(2,1)} %param.21) | copy-start | bytes 393220
  14.6 15.6 %copy-start.6 = (bf16[128,512]{1,0:T(8,128)(2,1)S(1)}, bf16[128,512]{1,0:T(8,128)(2,1)}, u32[]{:S(2)}) copy-start(bf16[128,512]{1,0:T(8,128)(2,1)} %param.22) | copy-start | bytes 393220
  14.6 16.4 %copy-start.8 = (bf16[128,512]{1,0:T(8,128)(2,1)S(1)}, bf16[128,512]{1,0:T(8,128)(2,1)}, u32[]{:S(2)}) copy-start(bf16[128,512]{1,0:T(8,128)(2,1)} %param.23) | copy-start | bytes 393220
  24.1 3.9 %copy-start.3 = (f32[384,512]{1,0:T(8,128)}, f32[384,512]{1,0:T(8,128)S(1)}, u32[]{:S(2)}) copy-start(f32[384,512]{1,0:T(8,128)S(1)} %scatter_custom_fusion) | copy-start | bytes 2359300
  24.1 7.1 %copy-start.15 = (s32[1,16]{1,0:T(1,128)S(1)}, s32[1,16]{1,0:T(1,128)}, u32[]{:S(2)}) copy-start(s32[1,16]{1,0:T(1,128)} %param.25) | copy-start | bytes 196
  24.9 254.8 %collective-permute-start.1 = (bf16[128,512]{1,0:T(8,128)(2,1)}, bf16[128,512]{1,0:T(8,128)(2,1)}, u32[]{:S(2)}, u32[]{:S(2)}) collective-permute-start(bf16[128,512]{1,0:T(8,128)(2,1)} %get-tuple-element.875), channel_id=1, source_target_pairs={{0,1},{1,2},{2,3},{3,4},{4,5},{5,6},{6,7},{7,8},{8,9},{9,10},{10,1... | collective-permute-start | bytes 393224 | tf_op jit(solution)/shard_map/ppermute | solution.py:18
  27.9 251.8 %collective-permute-start = (bf16[128,512]{1,0:T(8,128)(2,1)}, bf16[128,512]{1,0:T(8,128)(2,1)}, u32[]{:S(2)}, u32[]{:S(2)}) collective-permute-start(bf16[128,512]{1,0:T(8,128)(2,1)} %get-tuple-element.874), channel_id=1, source_target_pairs={{1,0},{2,1},{3,2},{4,3},{5,4},{6,5},{7,6},{8,7},{9,8},{10,9},{11,1... | collective-permute-start | bytes 393224 | tf_op jit(solution)/shard_map/ppermute | solution.py:18
  29.5 45.8 %copy-start.1 = (bf16[128,512]{0,1:T(8,128)(2,1)}, bf16[128,512]{0,1:T(8,128)(2,1)S(1)}, u32[]{:S(2)}) copy-start(bf16[128,512]{0,1:T(8,128)(2,1)S(1)} %copy.52) | copy-start | bytes 393220
  55.6 19.1 %copy-start.10 = (f32[128,8]{0,1:T(8,128)}, f32[128,8]{0,1:T(8,128)S(1)}, u32[]{:S(2)}) copy-start(f32[128,8]{0,1:T(8,128)S(1)} %fusion.70) | copy-start | bytes 12292
  159.8 25.8 %copy-start = (bf16[4,512,512]{1,2,0:T(8,128)(2,1)}, bf16[4,512,512]{1,2,0:T(8,128)(2,1)S(1)}, u32[]{:S(2)}) copy-start(bf16[4,512,512]{1,2,0:T(8,128)(2,1)S(1)} %get-tuple-element.1184) | copy-start | bytes 6291460
  159.8 25.8 %copy-start.9 = (pred[16]{0:T(512)(128)(4,1)}, pred[16]{0:T(512)(128)(4,1)S(1)}, u32[]{:S(2)}) copy-start(pred[16]{0:T(512)(128)(4,1)S(1)} %get-tuple-element.1201) | copy-start | bytes 52
  159.8 25.8 %copy-start.12 = (f32[128,8]{0,1:T(8,128)}, f32[128,8]{0,1:T(8,128)S(1)}, u32[]{:S(2)}) copy-start(f32[128,8]{0,1:T(8,128)S(1)} %log_add_fusion) | copy-start | bytes 12292
  240.4 2.4 copy-start.11
  250.8 2.4 copy-start.11
  250.8 2.4 copy-start.13
  261.1 2.4 copy-start.11
  271.4 2.4 copy-start.11
  271.4 2.4 copy-start.13
  (7 other events, 11.5 us)
Sparse Core Ops, SparseCore 0:
  10.2 44.2 all-gather.5
  56.6 40.0 all-gather.7
  98.9 40.1 all-gather.9
  141.1 40.2 all-gather.11
where the time goes:
time: 289 us; the launch traced here: 288 us
  blocking collectives  64.4 us (22%)
  waiting for transfers between devices  60 us (21%)
  local copies, waits for them, and re-layouts  49 us (17%)
  matrix products  45 us (16%)
  other arithmetic  34.5 us (12%)
  loops' own time  16.5 us (6%)
  between operations  14.1 us (5%)
  starting transfers between devices  4.43 us (2%)
    all_gather x1, waiting for transfers between devices, body(): lax.all_gather(queries, 'blk', axis=0, tiled=True)  38.2 us
    all_gather x1, blocking collectives, body(): lax.all_gather(block_mask, 'blk', axis=0, tiled=True)  24.4 us
    all_gather x1, blocking collectives, body(): lax.all_gather(log_total, 'blk', axis=0, tiled=True)  21.1 us
    dynamic_slice x24, local copies, waits for them, and re-layouts, blockwise(): lax.scan(advance, running, (jnp.arange(step_count, dtype=jnp.int32),) + s...  20.4 us
    all_gather x1, blocking collectives, body(): lax.all_gather(row_delta, 'blk', axis=0, tiled=True)  19 us
    unnamed x37, local copies, waits for them, and re-layouts  18.7 us
    all_gather x1, waiting for transfers between devices, body(): lax.all_gather(values, 'blk', axis=0, tiled=True)  18.7 us
    another operation x3, loops' own time, blockwise(): lax.scan(advance, running, (jnp.arange(step_count, dtype=jnp.int32),) + s...  15.9 us
  transfers between devices with their start and end apart: 6, of which 3 were waited for; matrix products, arithmetic and copies ran while one was open for 44% of the time, Pallas kernels for 0%

commit v1 on v0

v1 whole, which is shorter than its diff:
```python
import functools

import jax
import jax.numpy as jnp
from jax import lax
from jax.experimental import pallas as pl
from jax.experimental.pallas import tpu as pltpu
from jax.sharding import PartitionSpec as P

HEADS = 8
HD = 64
LANES = 128
F32 = jnp.float32
BF16 = jnp.bfloat16
NEG_LARGE = -1e30
NT = (((1,), (1,)), ((), ()))


def kernel(
    n,
    q_ref,
    k_ref,
    v_ref,
    o_ref,
    g_ref,
    mask_ref,
    nb_ref,
    cw_ref,
    dq_ref,
    dk_ref,
    dv_ref,
    kvs,
    qgs,
    sms,
    kv,
    qg,
    sm,
    kvt,
    w,
    bias,
    sbuf,
    dbuf,
    dsp,
    cvs,
    cvr,
    cvo,
    dqs,
    dqr,
    rds,
    rdr,
    outs,
    outr,
    kv_ss,
    kv_rs,
    qg_ss,
    qg_rs,
    sm_ss,
    sm_rs,
    fw_ss,
    fw_rs,
    cv_ss,
    cv_rs,
    dq_ss,
    dq_rs,
    rd_ss,
    rd_rs,
    out_ss,
    out_rs,
    lc_s,
):
    parts = n // HEADS
    rows = q_ref.shape[0]
    faces = nb_ref.shape[1]
    scale = HD**-0.5
    me = lax.axis_index("blk")
    head = me // parts
    part = me % parts

    def peer(d):
        return lax.rem(head + d, HEADS)

    def sibling(e):
        return lax.rem(part + e, parts)

    def at(index):
        return {"blk": index}

    above, below = lax.rem(me + n - 1, n), lax.rem(me + 1, n)

    barrier = pltpu.get_barrier_semaphore()
    partners = [peer(d) * parts + part for d in range(1, HEADS)]
    partners += [head * parts + sibling(e) for e in range(1, parts)]
    partners += [above, below]
    for other in partners:
        pl.semaphore_signal(barrier, inc=1, device_id=at(other), device_id_type=pl.DeviceIdType.MESH)

    def remote(src, dst, ss, rs, index):
        return pltpu.make_async_remote_copy(
            src_ref=src,
            dst_ref=dst,
            send_sem=ss,
            recv_sem=rs,
            device_id=at(index),
            device_id_type=pl.DeviceIdType.MESH,
        )

    for h in range(HEADS):
        cols = slice(h * HD, (h + 1) * HD)
        kvs[h] = jnp.concatenate([k_ref[:, cols], v_ref[:, cols]], axis=1)
        scaled = (q_ref[:, cols].astype(F32) * scale).astype(BF16)
        qgs[h] = jnp.concatenate([scaled, g_ref[:, cols]], axis=1)
    grads = g_ref[...].astype(F32)
    product = grads * o_ref[...].astype(F32)
    channels = product.shape[1]
    pick = (
        lax.broadcasted_iota(jnp.int32, (HEADS, channels), 1) // HD
        == lax.broadcasted_iota(jnp.int32, (HEADS, channels), 0)
    ).astype(F32)
    delta = lax.dot_general(
        pick, product, NT, precision=lax.Precision.HIGHEST, preferred_element_type=F32
    )
    mask_row = jnp.concatenate(
        [mask_ref[...].astype(F32), jnp.zeros((1, LANES - n), F32)], axis=1
    )
    sms[...] = jnp.zeros_like(sms)
    for h in range(HEADS):
        sms[h, 0:1, :] = delta[h : h + 1, :]
        sms[h, 1:2, :] = mask_row

    pl.semaphore_wait(barrier, len(partners))

    own = [
        pltpu.make_async_copy(kvs.at[head], kv.at[me], lc_s.at[0]),
        pltpu.make_async_copy(qgs.at[head], qg.at[head], lc_s.at[1]),
        pltpu.make_async_copy(sms.at[head], sm.at[head], lc_s.at[2]),
    ]
    kv_copies, qg_copies, sm_copies = [], [], []
    for d in range(1, HEADS):
        to, at_to = peer(d), peer(d) * parts + part
        kv_copies.append(
            remote(kvs.at[to], kv.at[me], kv_ss.at[d - 1], kv_rs.at[d - 1], at_to)
        )
        qg_copies.append(
            remote(qgs.at[to], qg.at[head], qg_ss.at[d - 1], qg_rs.at[d - 1], at_to)
        )
        sm_copies.append(
            remote(sms.at[to], sm.at[head], sm_ss.at[d - 1], sm_rs.at[d - 1], at_to)
        )
    for copy in own + kv_copies + qg_copies + sm_copies:
        copy.start()

    wide_nb = jnp.concatenate(
        [nb_ref[...].astype(F32), jnp.zeros((rows, LANES - faces), F32)], axis=1
    )
    turned = wide_nb.T.astype(jnp.int32)
    hits, terms = [], []
    for f in range(faces):
        line = turned[f : f + 1, :]
        where_to = jnp.where(line >= 0, line - me * rows + rows, -1)
        slots = lax.broadcasted_iota(jnp.int32, (3 * rows, rows), 0)
        hits.append((slots == where_to).astype(F32).astype(BF16))
        terms.append(grads * cw_ref[f : f + 1, :])
    hit = jnp.concatenate(hits, axis=1)
    term = jnp.concatenate(terms, axis=0)
    high = term.astype(BF16)
    low = (term - high.astype(F32)).astype(BF16)
    for b in range(3):
        block = hit[b * rows : (b + 1) * rows]
        spread = jnp.dot(block, high, preferred_element_type=F32) + jnp.dot(
            block, low, preferred_element_type=F32
        )
        if b == 1:
            cvo[...] = spread
        else:
            cvs[b // 2] = spread.astype(BF16)
    cv_copies = [
        remote(cvs.at[0], cvr.at[0], cv_ss.at[0], cv_rs.at[0], above),
        remote(cvs.at[1], cvr.at[1], cv_ss.at[1], cv_rs.at[1], below),
    ]
    for copy in cv_copies:
        copy.start()

    for copy in own:
        copy.wait()
    forwards = []
    for d in range(HEADS):
        source = lax.rem(head - d + HEADS, HEADS) * parts + part
        if d:
            kv_copies[d - 1].wait_recv()
        for e in range(1, parts):
            copy = remote(
                kv.at[source],
                kv.at[source],
                fw_ss.at[e - 1, d],
                fw_rs.at[e - 1, d],
                head * parts + sibling(e),
            )
            copy.start()
            forwards.append(copy)
    for copy in qg_copies + sm_copies:
        copy.wait_recv()
    first_half = lax.broadcasted_iota(jnp.int32, (rows, LANES), 1) < HD
    for i in range(HEADS):
        tile = qg[i].astype(F32)
        w[i * 2 * rows : i * 2 * rows + rows, :] = jnp.where(first_half, tile, 0.0).astype(BF16)
        w[i * 2 * rows + rows : (i + 1) * 2 * rows, :] = jnp.where(
            first_half, 0.0, tile
        ).astype(BF16)
    for copy in forwards:
        copy.wait_recv()

    def turn(j, carry):
        tile = kv[j].astype(F32).T
        kvt[:, pl.ds(pl.multiple_of(j * rows, rows), rows)] = tile[:HD].astype(BF16)
        return carry

    lax.fori_loop(0, n, turn, 0)

    chunk = 4
    chunks = n // chunk
    eye = lax.broadcasted_iota(jnp.int32, (n, LANES), 0) == lax.broadcasted_iota(
        jnp.int32, (n, LANES), 1
    )

    def dq_copy(t, i):
        return remote(
            dqs.at[t], dqr.at[head], dq_ss.at[t], dq_rs.at[t], i * parts + part
        )

    def queries_of(t, carry):
        i = lax.rem(head + t + 1, HEADS)
        w_i = w[pl.ds(pl.multiple_of(i * 2 * rows, 2 * rows), 2 * rows), :]
        delta_i = sm[i, 0:1, :]
        live = jnp.sum(jnp.where(eye, sm[i, 1:2, :], 0.0), axis=1, keepdims=True)
        bias[...] = jnp.broadcast_to((1.0 - live) * NEG_LARGE, (n, LANES))

        def scores(c, top):
            tile = kv[pl.ds(c * chunk, chunk)].reshape(chunk * rows, LANES)
            both = lax.dot_general(tile, w_i, NT, preferred_element_type=F32)
            for b in range(chunk):
                part_of = both[b * rows : (b + 1) * rows]
                s = part_of[:, :rows] + bias[pl.ds(c * chunk + b, 1), :]
                sbuf[c * chunk + b] = s
                dbuf[c * chunk + b] = part_of[:, rows:] - delta_i
                top = jnp.maximum(top, jnp.max(s.reshape(rows // 8, 8, rows), axis=0))
            return top

        top = lax.fori_loop(0, chunks, scores, jnp.full((8, rows), -jnp.inf, F32))
        top = jnp.max(top, axis=0, keepdims=True)

        def weigh(c, total):
            for b in range(chunk):
                e = jnp.exp(sbuf[c * chunk + b] - top)
                sbuf[c * chunk + b] = e
                total = total + jnp.sum(e.reshape(rows // 8, 8, rows), axis=0)
            return total

        total = lax.fori_loop(0, chunks, weigh, jnp.zeros((8, rows), F32))
        inverse = 1.0 / jnp.sum(total, axis=0, keepdims=True)
        left = pl.multiple_of(i * 2 * rows, 2 * rows)

        def combine(c, carry):
            for b in range(chunk):
                p = sbuf[c * chunk + b] * inverse
                ds = p * dbuf[c * chunk + b]
                dsp[c * chunk + b, :, pl.ds(left, rows)] = ds.astype(BF16)
                dsp[c * chunk + b, :, pl.ds(left + rows, rows)] = p.astype(BF16)
            return carry

        lax.fori_loop(0, chunks, combine, 0)
        ds_all = dsp[:, :, pl.ds(left, rows)].reshape(n * rows, rows)
        dq = jnp.dot(kvt[...], ds_all, preferred_element_type=F32) * scale

        @pl.when(t < HEADS - 1)
        def _():
            dqs[t] = dq.astype(BF16)
            dq_copy(t, i).start()

        @pl.when(t == HEADS - 1)
        def _():
            dqr[head] = dq.astype(BF16)

        return carry

    lax.fori_loop(0, HEADS, queries_of, 0)

    def key_sums(j):
        return jnp.dot(dsp[j], w[...], preferred_element_type=F32)

    def rd_copy(e, t):
        return remote(
            rds.at[e - 1, t],
            rdr.at[e - 1, t],
            rd_ss.at[e - 1, t],
            rd_rs.at[e - 1, t],
            head * parts + sibling(e),
        )

    for e in range(1, parts):

        def for_sibling(t, carry, e=e):
            rds[e - 1, t] = key_sums(t * parts + sibling(e))
            rd_copy(e, t).start()
            return carry

        lax.fori_loop(0, HEADS, for_sibling, 0)

    def out_copy(t, i):
        return remote(
            outs.at[t], outr.at[head], out_ss.at[t], out_rs.at[t], i * parts + part
        )

    def for_owner(t, carry):
        i = lax.rem(head + t + 1, HEADS)
        total = key_sums(i * parts + part)
        for e in range(1, parts):
            rd_copy(e, i).wait_recv()
            total = total + rdr[e - 1, i]

        @pl.when(t < HEADS - 1)
        def _():
            outs[t] = total.astype(BF16)
            out_copy(t, i).start()

        @pl.when(t == HEADS - 1)
        def _():
            outr[head] = total.astype(BF16)

        return carry

    lax.fori_loop(0, HEADS, for_owner, 0)

    for t in range(HEADS - 1):
        dq_copy(t, 0).wait_recv()
    turned_dq = dqr[...].astype(F32).reshape(HEADS * HD, rows).T
    dq_ref[...] = turned_dq.astype(BF16)
    for copy in cv_copies:
        copy.wait_recv()
    conv = cvo[...] + cvr[0].astype(F32) + cvr[1].astype(F32)
    for t in range(HEADS - 1):
        out_copy(t, 0).wait_recv()
    tiles = [outr[h].astype(F32) for h in range(HEADS)]
    dk_ref[...] = jnp.concatenate([tile[:, :HD] for tile in tiles], axis=1).astype(BF16)
    dv_ref[...] = (jnp.concatenate([tile[:, HD:] for tile in tiles], axis=1) + conv).astype(BF16)

    for copy in kv_copies + qg_copies + sm_copies + cv_copies + forwards:
        copy.wait_send()
    for t in range(HEADS - 1):
        dq_copy(t, 0).wait_send()
        out_copy(t, 0).wait_send()
    for e in range(1, parts):
        for t in range(HEADS):
            rd_copy(e, t).wait_send()


def body(queries, keys, values, outputs, grad_out, block_mask, neighbours, conv_weight):
    n = lax.axis_size("blk")
    rows, channels = queries.shape
    parts = n // HEADS
    dma = pltpu.SemaphoreType.DMA
    vmem = pl.BlockSpec(memory_space=pltpu.VMEM)
    shape = jax.ShapeDtypeStruct((rows, channels), BF16)
    others = HEADS - 1
    return pl.pallas_call(
        functools.partial(kernel, n),
        out_shape=(shape, shape, shape),
        in_specs=[vmem] * 8,
        out_specs=(vmem, vmem, vmem),
        scratch_shapes=[
            pltpu.VMEM((HEADS, rows, LANES), BF16),
            pltpu.VMEM((HEADS, rows, LANES), BF16),
            pltpu.VMEM((HEADS, 8, LANES), F32),
            pltpu.VMEM((n, rows, LANES), BF16),
            pltpu.VMEM((HEADS, rows, LANES), BF16),
            pltpu.VMEM((HEADS, 8, LANES), F32),
            pltpu.VMEM((HD, n * rows), BF16),
            pltpu.VMEM((HEADS * 2 * rows, LANES), BF16),
            pltpu.VMEM((n, LANES), F32),
            pltpu.VMEM((n, rows, rows), F32),
            pltpu.VMEM((n, rows, rows), F32),
            pltpu.VMEM((n, rows, HEADS * 2 * rows), BF16),
            pltpu.VMEM((2, rows, channels), BF16),
            pltpu.VMEM((2, rows, channels), BF16),
            pltpu.VMEM((rows, channels), F32),
            pltpu.VMEM((HEADS, HD, rows), BF16),
            pltpu.VMEM((HEADS, HD, rows), BF16),
            pltpu.VMEM((parts - 1, HEADS, rows, LANES), F32),
            pltpu.VMEM((parts - 1, HEADS, rows, LANES), F32),
            pltpu.VMEM((HEADS, rows, LANES), BF16),
            pltpu.VMEM((HEADS, rows, LANES), BF16),
            dma((others,)),
            dma((others,)),
            dma((others,)),
            dma((others,)),
            dma((others,)),
            dma((others,)),
            dma((parts - 1, HEADS)),
            dma((parts - 1, HEADS)),
            dma((2,)),
            dma((2,)),
            dma((others,)),
            dma((others,)),
            dma((parts - 1, HEADS)),
            dma((parts - 1, HEADS)),
            dma((others,)),
            dma((others,)),
            dma((3,)),
        ],
        compiler_params=pltpu.CompilerParams(
            collective_id=0, has_side_effects=True, vmem_limit_bytes=60 * 2**20
        ),
    )(queries, keys, values, outputs, grad_out, block_mask, neighbours, conv_weight)


def solution(mesh):
    tokens = P(("group", "blk"), None)
    return jax.shard_map(
        body,
        mesh=mesh,
        in_specs=(tokens,) * 7 + (P(),),
        out_specs=(tokens,) * 3,
        check_vma=False,
    )
```

time: 289 us -> 55.3 us (0.19)
  blocking collectives: 64.4 us -> 0 us
  waiting for transfers between devices: 60 us -> 0 us
  Pallas kernels: 0 us -> 49.8 us
  matrix products: 45 us -> 0 us
  local copies, waits for them, and re-layouts: 49 us -> 4.63 us
  other arithmetic: 34.5 us -> 0 us
  loops' own time: 16.5 us -> 0 us
  between operations: 14.1 us -> 0.65 us
  starting transfers between devices: 4.43 us -> 0 us
    all_gather x3 -> x0, blocking collectives: 64.4 us -> none  [the longest x1 24.4 us: body(): lax.all_gather(block_mask, 'blk', axis=0, tiled=True)]
    all_gather x4 -> x0, waiting for transfers between devices: 57.5 us -> none  [the longest x1 38.2 us: body(): lax.all_gather(queries, 'blk', axis=0, tiled=True)]
    pallas_call x0 -> x1, Pallas kernels: none -> 49.8 us  [body(): pl.pallas_call(functools.partial(kernel, n), out_shape=(shape, shape, sha...]
    dot_general x28 -> x0, matrix products: 45 us -> none  [the longest x4 13 us: query_terms(): jnp.einsum('ths,shd->thd', grad_score, key_wide, precision=highest)]
    dynamic_slice x28 -> x0, local copies, waits for them, and re-layouts: 26.1 us -> none  [the longest x24 20.4 us: blockwise(): lax.scan(advance, running, (jnp.arange(step_count, dtype=jnp.int32),) + s...]
    another operation x15 -> x0, loops' own time: 16.5 us -> none  [the longest x3 15.9 us: blockwise(): lax.scan(advance, running, (jnp.arange(step_count, dtype=jnp.int32),) + s...]
    unnamed x37 -> x8, local copies, waits for them, and re-layouts: 18.7 us -> 4.63 us
    and x12 -> x0, other arithmetic: 13.9 us -> none  [the longest x8 8.51 us: live_keys(): (owners[:, None] == block_ids[None, :]) & mask_line[None, :]]
  transfers between devices with their start and end apart: 6 -> 0, of which waited for: 3 -> 0; matrix products, arithmetic and copies ran while one was open for 44% -> 0% of each run, Pallas kernels for 0% -> 0%
where the time goes in v1:
time: 55.3 us; the launch traced here: 55.1 us
  Pallas kernels  49.8 us (90%)
  local copies, waits for them, and re-layouts  4.63 us (8%)
  between operations  0.65 us (1%)
    pallas_call x1, Pallas kernels, body(): pl.pallas_call(functools.partial(kernel, n), out_shape=(shape, shape, sha...  49.8 us
    unnamed x8, local copies, waits for them, and re-layouts  4.63 us

profile of v1, /device:TPU:0, one launch (start us, length us, event | category | flops | bytes accessed | tf_op | source)
XLA Modules:
  0.0 55.1 jit_solution(7213079868883000722)
XLA Ops:
  0.6 1.4 %copy.11.nb_ref = s32[128,6]{1,0:T(8,128)} copy(s32[128,6]{0,1:T(8,128)} %param.14) | data formatting | bytes 6144 | tf_op args[6]
  2.1 49.8 %shard_map.103 = (bf16[128,512]{1,0:T(8,128)(2,1)}, bf16[128,512]{1,0:T(8,128)(2,1)}, bf16[128,512]{1,0:T(8,128)(2,1)}) custom-call(bf16[128,512]{1,0:T(8,128)(2,1)} %q_ref.1, bf16[128,512]{1,0:T(8,128)(2,1)} %k_ref.1, bf16[128,512]{1,0:T(8,128)(2,1)} %v_ref.1, bf16[128,512]{1,0:T(8,128)(2,1)} %o_ref.1, bf16[128,512]{1,0:T(8,128)(2,1)} %g_ref.1, ...), custom_call_target="tpu_custom_call" | custom-call | tf_op jit(solution)/shard_map/pallas_call | solution.py:364
  51.9 0.0 copy-start.1
  51.9 1.6 %copy.15 = bf16[128,512]{1,0:T(8,128)(2,1)} copy(bf16[128,512]{1,0:T(8,128)(2,1)} %get-tuple-element.6) | data formatting | bytes 262144
  53.5 0.0 copy-done.1
  53.5 0.0 copy-start
  53.5 0.7 %copy.16 = bf16[128,512]{1,0:T(8,128)(2,1)} copy(bf16[128,512]{1,0:T(8,128)(2,1)S(1)} %copy-done.1) | data formatting | bytes 262144
  54.2 0.3 copy-done
  54.5 0.7 %copy.17 = bf16[128,512]{1,0:T(8,128)(2,1)} copy(bf16[128,512]{1,0:T(8,128)(2,1)S(1)} %copy-done) | data formatting | bytes 262144
Async XLA Ops:
  51.9 1.6 %copy-start.1 = (bf16[128,512]{1,0:T(8,128)(2,1)S(1)}, bf16[128,512]{1,0:T(8,128)(2,1)}, u32[]{:S(2)}) copy-start(bf16[128,512]{1,0:T(8,128)(2,1)} %get-tuple-element.7) | copy-start | bytes 393220
  53.5 1.0 %copy-start = (bf16[128,512]{1,0:T(8,128)(2,1)S(1)}, bf16[128,512]{1,0:T(8,128)(2,1)}, u32[]{:S(2)}) copy-start(bf16[128,512]{1,0:T(8,128)(2,1)} %get-tuple-element.8) | copy-start | bytes 393220

commit v2 on v1

v2 whole, which is shorter than its diff:
```python
import functools

import jax
import jax.numpy as jnp
from jax import lax
from jax.experimental import pallas as pl
from jax.experimental.pallas import tpu as pltpu
from jax.sharding import PartitionSpec as P

HEADS = 8
HD = 64
LANES = 128
F32 = jnp.float32
BF16 = jnp.bfloat16
NEG_LARGE = -1e30
NT = (((1,), (1,)), ((), ()))


def kernel(
    n,
    early,
    q_ref,
    k_ref,
    v_ref,
    o_ref,
    g_ref,
    mask_ref,
    nb_ref,
    cw_ref,
    dq_ref,
    dk_ref,
    dv_ref,
    kvs,
    qgs,
    sms,
    kv,
    qg,
    sm,
    kvt,
    w,
    add,
    tops,
    sbuf,
    dsp,
    dkv,
    cvs,
    cvr,
    cvo,
    dqs,
    dqr,
    rds,
    rdr,
    outs,
    outr,
    kv_ss,
    kv_rs,
    qg_ss,
    qg_rs,
    sm_ss,
    sm_rs,
    fw_ss,
    fw_rs,
    cv_ss,
    cv_rs,
    dq_ss,
    dq_rs,
    rd_ss,
    rd_rs,
    out_ss,
    out_rs,
    lc_s,
):
    parts = n // HEADS
    rows = q_ref.shape[0]
    faces = nb_ref.shape[0]
    scale = HD**-0.5
    me = lax.axis_index("blk")
    head = me // parts
    part = me % parts

    def peer(d):
        return lax.rem(head + d, HEADS)

    def sibling(e):
        return lax.rem(part + e, parts)

    def at(index):
        return {"blk": index}

    above, below = lax.rem(me + n - 1, n), lax.rem(me + 1, n)

    barrier = pltpu.get_barrier_semaphore()
    partners = [peer(d) * parts + part for d in range(1, HEADS)]
    partners += [head * parts + sibling(e) for e in range(1, parts)]
    partners += [above, below]
    for other in partners:
        pl.semaphore_signal(barrier, inc=1, device_id=at(other), device_id_type=pl.DeviceIdType.MESH)

    def remote(src, dst, ss, rs, index):
        return pltpu.make_async_remote_copy(
            src_ref=src,
            dst_ref=dst,
            send_sem=ss,
            recv_sem=rs,
            device_id=at(index),
            device_id_type=pl.DeviceIdType.MESH,
        )

    for h in range(HEADS):
        cols = slice(h * HD, (h + 1) * HD)
        scaled = (q_ref[:, cols].astype(F32) * scale).astype(BF16)
        qgs[h] = jnp.concatenate([scaled, g_ref[:, cols]], axis=1)
    sms[...] = jnp.zeros_like(sms)

    pl.semaphore_wait(barrier, len(partners))

    def exchange(buffer, target, ss, rs):
        copies = [
            remote(buffer.at[peer(d)], target, ss.at[d - 1], rs.at[d - 1], peer(d) * parts + part)
            for d in range(1, HEADS)
        ]
        for copy in copies:
            copy.start()
        return copies

    own = [
        pltpu.make_async_copy(kvs.at[head], kv.at[me], lc_s.at[0]),
        pltpu.make_async_copy(qgs.at[head], qg.at[head], lc_s.at[1]),
        pltpu.make_async_copy(sms.at[head], sm.at[head], lc_s.at[2]),
    ]
    own[1].start()
    qg_copies = exchange(qgs, qg.at[head], qg_ss, qg_rs)
    for h in range(HEADS):
        cols = slice(h * HD, (h + 1) * HD)
        kvs[h] = jnp.concatenate([k_ref[:, cols], v_ref[:, cols]], axis=1)
    own[0].start()
    kv_copies = exchange(kvs, kv.at[me], kv_ss, kv_rs)

    grads = g_ref[...].astype(F32)
    product = grads * o_ref[...].astype(F32)
    channels = product.shape[1]
    pick = (
        lax.broadcasted_iota(jnp.int32, (HEADS, channels), 1) // HD
        == lax.broadcasted_iota(jnp.int32, (HEADS, channels), 0)
    ).astype(F32)
    delta = lax.dot_general(
        pick, product, NT, precision=lax.Precision.HIGHEST, preferred_element_type=F32
    )
    mask_row = jnp.concatenate(
        [mask_ref[...].astype(F32), jnp.zeros((1, LANES - n), F32)], axis=1
    )
    for h in range(HEADS):
        sms[h, 0:1, :] = delta[h : h + 1, :]
        sms[h, 1:2, :] = mask_row
    own[2].start()
    sm_copies = exchange(sms, sm.at[head], sm_ss, sm_rs)

    hits, terms = [], []
    for f in range(faces):
        line = nb_ref[f : f + 1, :]
        where_to = jnp.where(line >= 0, line - me * rows + rows, -1)
        slots = lax.broadcasted_iota(jnp.int32, (3 * rows, rows), 0)
        hits.append((slots == where_to).astype(F32).astype(BF16))
        terms.append(grads * cw_ref[f : f + 1, :])
    hit = jnp.concatenate(hits, axis=1)
    term = jnp.concatenate(terms, axis=0)
    high = term.astype(BF16)
    low = (term - high.astype(F32)).astype(BF16)
    for b in range(3):
        block = hit[b * rows : (b + 1) * rows]
        spread = jnp.dot(block, high, preferred_element_type=F32) + jnp.dot(
            block, low, preferred_element_type=F32
        )
        if b == 1:
            cvo[...] = spread
        else:
            cvs[b // 2] = spread.astype(BF16)
    cv_copies = [
        remote(cvs.at[0], cvr.at[0], cv_ss.at[0], cv_rs.at[0], above),
        remote(cvs.at[1], cvr.at[1], cv_ss.at[1], cv_rs.at[1], below),
    ]
    for copy in cv_copies:
        copy.start()

    pair = 4 * rows
    for copy in own:
        copy.wait()
    for copy in qg_copies + sm_copies:
        copy.wait_recv()
    first_half = lax.broadcasted_iota(jnp.int32, (rows, LANES), 1) < HD
    eye = lax.broadcasted_iota(jnp.int32, (n, LANES), 0) == lax.broadcasted_iota(
        jnp.int32, (n, LANES), 1
    )
    for i in range(HEADS):
        tile = qg[i].astype(F32)
        at_q = i // 2 * pair + i % 2 * rows
        at_g = at_q + 2 * rows
        w[at_q : at_q + rows, :] = jnp.where(first_half, tile, 0.0).astype(BF16)
        w[at_g : at_g + rows, :] = jnp.where(first_half, 0.0, tile).astype(BF16)
        live = jnp.sum(jnp.where(eye, sm[i, 1:2, :], 0.0), axis=1, keepdims=True)
        add[:, at_q : at_q + rows] = jnp.broadcast_to((1.0 - live) * NEG_LARGE, (n, rows))
        add[:, at_g : at_g + rows] = jnp.broadcast_to(-sm[i, 0:1, :], (n, rows))
    tops[...] = jnp.full_like(tops, -jnp.inf)

    def score(js, a, w_a):
        lhs = jnp.concatenate([kv[j] for j in js], axis=0)
        both = lax.dot_general(lhs, w_a, NT, preferred_element_type=F32)
        slot = a if early else 0
        top = tops[a]
        for b, j in enumerate(js):
            tile = both[b * rows : (b + 1) * rows] + add[pl.ds(j, 1), pl.ds(a * pair, pair)]
            sbuf[slot, j] = tile
            s = tile[:, : 2 * rows]
            top = jnp.maximum(top, jnp.max(s.reshape(rows // 8, 8, 2 * rows), axis=0))
        tops[a] = top

    def turn(j):
        tile = kv[j].astype(F32).T
        kvt[:, pl.ds(pl.multiple_of(j * rows, rows), rows)] = tile[:HD].astype(BF16)

    def arrived(js):
        for j in js:
            turn(j)
        if early:
            for a in range(HEADS // 2):
                score(js, a, w[a * pair : (a + 1) * pair, :])

    forwards = []
    waiting = []
    for d in range(HEADS + 1):
        js = []
        ready = waiting
        waiting = []
        if d < HEADS:
            chip = lax.rem(head - d + HEADS, HEADS)
            source = chip * parts + part
            if d:
                kv_copies[d - 1].wait_recv()
            for e in range(1, parts):
                copy = remote(
                    kv.at[source],
                    kv.at[source],
                    fw_ss.at[e - 1, d],
                    fw_rs.at[e - 1, d],
                    head * parts + sibling(e),
                )
                copy.start()
                forwards.append(copy)
                waiting.append((copy, chip * parts + lax.rem(part - e + parts, parts)))
            js.append(source)
        for copy, j in ready:
            copy.wait_recv()
            js.append(j)
        arrived(js)

    chunk = 2
    chunks = n // chunk

    def dq_copy(i, u):
        return remote(dqs.at[i], dqr.at[head], dq_ss.at[i], dq_rs.at[u], i * parts + part)

    def pair_of(t, carry):
        a = lax.rem(head // 2 + t + 1, HEADS // 2)
        at_a = pl.multiple_of(a * pair, pair)
        w_a = w[pl.ds(at_a, pair), :]
        slot = a if early else 0
        left = at_a if early else 0
        if not early:

            def scores(c, carry):
                score([c * chunk + b for b in range(chunk)], a, w_a)
                return carry

            lax.fori_loop(0, chunks, scores, 0)
        top = jnp.max(tops[a], axis=0, keepdims=True)

        def weigh(c, total):
            for b in range(chunk):
                e = jnp.exp(sbuf[slot, c * chunk + b, :, : 2 * rows] - top)
                sbuf[slot, c * chunk + b, :, : 2 * rows] = e
                total = total + jnp.sum(e.reshape(rows // 8, 8, 2 * rows), axis=0)
            return total

        total = lax.fori_loop(0, chunks, weigh, jnp.zeros((8, 2 * rows), F32))
        inverse = 1.0 / jnp.sum(total, axis=0, keepdims=True)

        def combine(c, carry):
            for b in range(chunk):
                j = c * chunk + b
                p = sbuf[slot, j, :, : 2 * rows] * inverse
                ds = p * sbuf[slot, j, :, 2 * rows :]
                dsp[j, :, pl.ds(left, 2 * rows)] = ds.astype(BF16)
                dsp[j, :, pl.ds(left + 2 * rows, 2 * rows)] = p.astype(BF16)
            return carry

        lax.fori_loop(0, chunks, combine, 0)
        ds_all = dsp[:, :, pl.ds(left, 2 * rows)].reshape(n * rows, 2 * rows)
        dq = (jnp.dot(kvt[...], ds_all, preferred_element_type=F32) * scale).astype(BF16)
        for u in range(2):
            i = 2 * a + u
            block = dq[:, u * rows : (u + 1) * rows]

            @pl.when(i != head)
            def _():
                dqs[i] = block
                dq_copy(i, head).start()

            @pl.when(i == head)
            def _():
                dqr[head] = block

        if not early:

            def gather(j, carry):
                term = jnp.dot(dsp[j], w_a, preferred_element_type=F32)
                dkv[j] = jnp.where(t == 0, term, dkv[j] + term)
                return carry

            lax.fori_loop(0, n, gather, 0)
        return carry

    lax.fori_loop(0, HEADS // 2, pair_of, 0)

    def key_sums(j):
        if not early:
            return dkv[j]
        return jnp.dot(dsp[j], w[...], preferred_element_type=F32)

    def rd_copy(e, t):
        return remote(
            rds.at[e - 1, t],
            rdr.at[e - 1, t],
            rd_ss.at[e - 1, t],
            rd_rs.at[e - 1, t],
            head * parts + sibling(e),
        )

    for e in range(1, parts):

        def for_sibling(t, carry, e=e):
            rds[e - 1, t] = key_sums(t * parts + sibling(e))
            rd_copy(e, t).start()
            return carry

        lax.fori_loop(0, HEADS, for_sibling, 0)

    def out_copy(t, i):
        return remote(
            outs.at[t], outr.at[head], out_ss.at[t], out_rs.at[t], i * parts + part
        )

    def for_owner(t, carry):
        i = lax.rem(head + t + 1, HEADS)
        total = key_sums(i * parts + part)
        for e in range(1, parts):
            rd_copy(e, i).wait_recv()
            total = total + rdr[e - 1, i]

        @pl.when(t < HEADS - 1)
        def _():
            outs[t] = total.astype(BF16)
            out_copy(t, i).start()

        @pl.when(t == HEADS - 1)
        def _():
            outr[head] = total.astype(BF16)

        return carry

    lax.fori_loop(0, HEADS, for_owner, 0)

    for d in range(1, HEADS):
        dq_copy(peer(d), peer(d)).wait_recv()
    turned_dq = dqr[...].astype(F32).reshape(HEADS * HD, rows).T
    dq_ref[...] = turned_dq.astype(BF16)
    for copy in cv_copies:
        copy.wait_recv()
    conv = cvo[...] + cvr[0].astype(F32) + cvr[1].astype(F32)
    for t in range(HEADS - 1):
        out_copy(t, 0).wait_recv()
    tiles = [outr[h].astype(F32) for h in range(HEADS)]
    dk_ref[...] = jnp.concatenate([tile[:, :HD] for tile in tiles], axis=1).astype(BF16)
    dv_ref[...] = (jnp.concatenate([tile[:, HD:] for tile in tiles], axis=1) + conv).astype(BF16)

    for copy in kv_copies + qg_copies + sm_copies + cv_copies + forwards:
        copy.wait_send()
    for t in range(HEADS - 1):
        dq_copy(peer(t + 1), 0).wait_send()
        out_copy(t, 0).wait_send()
    for e in range(1, parts):
        for t in range(HEADS):
            rd_copy(e, t).wait_send()


def body(queries, keys, values, outputs, grad_out, block_mask, neighbours, conv_weight):
    n = lax.axis_size("blk")
    rows, channels = queries.shape
    parts = n // HEADS
    early = n * rows * rows * HEADS * 8 <= 20 * 2**20
    dma = pltpu.SemaphoreType.DMA
    vmem = pl.BlockSpec(memory_space=pltpu.VMEM)
    shape = jax.ShapeDtypeStruct((rows, channels), BF16)
    others = HEADS - 1
    return pl.pallas_call(
        functools.partial(kernel, n, early),
        out_shape=(shape, shape, shape),
        in_specs=[vmem] * 8,
        out_specs=(vmem, vmem, vmem),
        scratch_shapes=[
            pltpu.VMEM((HEADS, rows, LANES), BF16),
            pltpu.VMEM((HEADS, rows, LANES), BF16),
            pltpu.VMEM((HEADS, 8, LANES), F32),
            pltpu.VMEM((n, rows, LANES), BF16),
            pltpu.VMEM((HEADS, rows, LANES), BF16),
            pltpu.VMEM((HEADS, 8, LANES), F32),
            pltpu.VMEM((HD, n * rows), BF16),
            pltpu.VMEM((HEADS * 2 * rows, LANES), BF16),
            pltpu.VMEM((n, HEADS * 2 * rows), F32),
            pltpu.VMEM((HEADS // 2, 8, 2 * rows), F32),
            pltpu.VMEM((HEADS // 2 if early else 1, n, rows, 4 * rows), F32),
            pltpu.VMEM((n, rows, (HEADS * 2 if early else 4) * rows), BF16),
            pltpu.VMEM((8, LANES) if early else (n, rows, LANES), F32),
            pltpu.VMEM((2, rows, channels), BF16),
            pltpu.VMEM((2, rows, channels), BF16),
            pltpu.VMEM((rows, channels), F32),
            pltpu.VMEM((HEADS, HD, rows), BF16),
            pltpu.VMEM((HEADS, HD, rows), BF16),
            pltpu.VMEM((parts - 1, HEADS, rows, LANES), F32),
            pltpu.VMEM((parts - 1, HEADS, rows, LANES), F32),
            pltpu.VMEM((HEADS, rows, LANES), BF16),
            pltpu.VMEM((HEADS, rows, LANES), BF16),
            dma((others,)),
            dma((others,)),
            dma((others,)),
            dma((others,)),
            dma((others,)),
            dma((others,)),
            dma((parts - 1, HEADS)),
            dma((parts - 1, HEADS)),
            dma((2,)),
            dma((2,)),
            dma((HEADS,)),
            dma((HEADS,)),
            dma((parts - 1, HEADS)),
            dma((parts - 1, HEADS)),
            dma((others,)),
            dma((others,)),
            dma((3,)),
        ],
        compiler_params=pltpu.CompilerParams(
            collective_id=0, has_side_effects=True, vmem_limit_bytes=60 * 2**20
        ),
    )(queries, keys, values, outputs, grad_out, block_mask, neighbours.T, conv_weight)


def solution(mesh):
    tokens = P(("group", "blk"), None)
    return jax.shard_map(
        body,
        mesh=mesh,
        in_specs=(tokens,) * 7 + (P(),),
        out_specs=(tokens,) * 3,
        check_vma=False,
    )
```

time: 55.3 us -> 48.1 us (0.87)
  Pallas kernels: 49.8 us -> 44.1 us
  local copies, waits for them, and re-layouts: 4.63 us -> 3.21 us
    pallas_call x1, Pallas kernels: 49.8 us -> 44.1 us  [body(): pl.pallas_call(functools.partial(kernel, n, early), out_shape=(shape, sha...]
    unnamed x8 -> x7, local copies, waits for them, and re-layouts: 4.63 us -> 3.21 us
where the time goes in v2:
time: 48.1 us; the launch traced here: 47.9 us
  Pallas kernels  44.1 us (92%)
  local copies, waits for them, and re-layouts  3.21 us (7%)
  between operations  0.65 us (1%)
    pallas_call x1, Pallas kernels, body(): pl.pallas_call(functools.partial(kernel, n, early), out_shape=(shape, sha...  44.1 us
    unnamed x7, local copies, waits for them, and re-layouts  3.21 us

profile of v2, /device:TPU:0, one launch (start us, length us, event | category | flops | bytes accessed | tf_op | source)
XLA Modules:
  0.0 47.9 jit_solution(13277264931608909556)
XLA Ops:
  0.6 44.1 %shard_map.103 = (bf16[128,512]{1,0:T(8,128)(2,1)}, bf16[128,512]{1,0:T(8,128)(2,1)}, bf16[128,512]{1,0:T(8,128)(2,1)}) custom-call(bf16[128,512]{1,0:T(8,128)(2,1)} %q_ref.1, bf16[128,512]{1,0:T(8,128)(2,1)} %k_ref.1, bf16[128,512]{1,0:T(8,128)(2,1)} %v_ref.1, bf16[128,512]{1,0:T(8,128)(2,1)} %o_ref.1, bf16[128,512]{1,0:T(8,128)(2,1)} %g_ref.1, ...), custom_call_target="tpu_custom_call" | custom-call | tf_op jit(solution)/shard_map/pallas_call | solution.py:404
  44.7 0.0 copy-start.1
  44.7 1.6 %copy.14 = bf16[128,512]{1,0:T(8,128)(2,1)} copy(bf16[128,512]{1,0:T(8,128)(2,1)} %get-tuple-element.6) | data formatting | bytes 262144
  46.3 0.0 copy-done.1
  46.3 0.0 copy-start
  46.3 0.7 %copy.15 = bf16[128,512]{1,0:T(8,128)(2,1)} copy(bf16[128,512]{1,0:T(8,128)(2,1)S(1)} %copy-done.1) | data formatting | bytes 262144
  47.0 0.3 copy-done
  47.3 0.7 %copy.16 = bf16[128,512]{1,0:T(8,128)(2,1)} copy(bf16[128,512]{1,0:T(8,128)(2,1)S(1)} %copy-done) | data formatting | bytes 262144
Async XLA Ops:
  44.7 1.6 %copy-start.1 = (bf16[128,512]{1,0:T(8,128)(2,1)S(1)}, bf16[128,512]{1,0:T(8,128)(2,1)}, u32[]{:S(2)}) copy-start(bf16[128,512]{1,0:T(8,128)(2,1)} %get-tuple-element.7) | copy-start | bytes 393220
  46.3 1.0 %copy-start = (bf16[128,512]{1,0:T(8,128)(2,1)S(1)}, bf16[128,512]{1,0:T(8,128)(2,1)}, u32[]{:S(2)}) copy-start(bf16[128,512]{1,0:T(8,128)(2,1)} %get-tuple-element.8) | copy-start | bytes 393220

commit v3 on v2

--- a/solution.py
+++ b/solution.py
@@ -28,8 +28,8 @@
     nb_ref,
     cw_ref,
     dq_ref,
-    dk_ref,
-    dv_ref,
+    out_ref,
+    conv_ref,
     kvs,
     qgs,
     sms,
@@ -111,31 +111,9 @@
         scaled = (q_ref[:, cols].astype(F32) * scale).astype(BF16)
         qgs[h] = jnp.concatenate([scaled, g_ref[:, cols]], axis=1)
     sms[...] = jnp.zeros_like(sms)
-
-    pl.semaphore_wait(barrier, len(partners))
-
-    def exchange(buffer, target, ss, rs):
-        copies = [
-            remote(buffer.at[peer(d)], target, ss.at[d - 1], rs.at[d - 1], peer(d) * parts + part)
-            for d in range(1, HEADS)
-        ]
-        for copy in copies:
-            copy.start()
-        return copies
-
-    own = [
-        pltpu.make_async_copy(kvs.at[head], kv.at[me], lc_s.at[0]),
-        pltpu.make_async_copy(qgs.at[head], qg.at[head], lc_s.at[1]),
-        pltpu.make_async_copy(sms.at[head], sm.at[head], lc_s.at[2]),
-    ]
-    own[1].start()
-    qg_copies = exchange(qgs, qg.at[head], qg_ss, qg_rs)
     for h in range(HEADS):
         cols = slice(h * HD, (h + 1) * HD)
         kvs[h] = jnp.concatenate([k_ref[:, cols], v_ref[:, cols]], axis=1)
-    own[0].start()
-    kv_copies = exchange(kvs, kv.at[me], kv_ss, kv_rs)
-
     grads = g_ref[...].astype(F32)
     product = grads * o_ref[...].astype(F32)
     channels = product.shape[1]
@@ -152,8 +130,28 @@
     for h in range(HEADS):
         sms[h, 0:1, :] = delta[h : h + 1, :]
         sms[h, 1:2, :] = mask_row
-    own[2].start()
+
+    pl.semaphore_wait(barrier, len(partners))
+
+    def exchange(buffer, target, ss, rs):
+        copies = [
+            remote(buffer.at[peer(d)], target, ss.at[d - 1], rs.at[d - 1], peer(d) * parts + part)
+            for d in range(1, HEADS)
+        ]
+        for copy in copies:
+            copy.start()
+        return copies
+
+    own = [
+        pltpu.make_async_copy(kvs.at[head], kv.at[me], lc_s.at[0]),
+        pltpu.make_async_copy(qgs.at[head], qg.at[head], lc_s.at[1]),
+        pltpu.make_async_copy(sms.at[head], sm.at[head], lc_s.at[2]),
+    ]
+    for copy in own:
+        copy.start()
     sm_copies = exchange(sms, sm.at[head], sm_ss, sm_rs)
+    qg_copies = exchange(qgs, qg.at[head], qg_ss, qg_rs)
+    kv_copies = exchange(kvs, kv.at[me], kv_ss, kv_rs)
 
     hits, terms = [], []
     for f in range(faces):
@@ -179,8 +177,6 @@
         remote(cvs.at[0], cvr.at[0], cv_ss.at[0], cv_rs.at[0], above),
         remote(cvs.at[1], cvr.at[1], cv_ss.at[1], cv_rs.at[1], below),
     ]
-    for copy in cv_copies:
-        copy.start()
 
     pair = 4 * rows
     for copy in own:
@@ -253,6 +249,9 @@
             js.append(j)
         arrived(js)
 
+    for copy in cv_copies:
+        copy.start()
+
     chunk = 2
     chunks = n // chunk
 
@@ -371,16 +370,13 @@
 
     for d in range(1, HEADS):
         dq_copy(peer(d), peer(d)).wait_recv()
-    turned_dq = dqr[...].astype(F32).reshape(HEADS * HD, rows).T
-    dq_ref[...] = turned_dq.astype(BF16)
+    dq_ref[...] = dqr[...]
     for copy in cv_copies:
         copy.wait_recv()
-    conv = cvo[...] + cvr[0].astype(F32) + cvr[1].astype(F32)
+    conv_ref[...] = cvo[...] + cvr[0].astype(F32) + cvr[1].astype(F32)
     for t in range(HEADS - 1):
         out_copy(t, 0).wait_recv()
-    tiles = [outr[h].astype(F32) for h in range(HEADS)]
-    dk_ref[...] = jnp.concatenate([tile[:, :HD] for tile in tiles], axis=1).astype(BF16)
-    dv_ref[...] = (jnp.concatenate([tile[:, HD:] for tile in tiles], axis=1) + conv).astype(BF16)
+    out_ref[...] = outr[...]
 
     for copy in kv_copies + qg_copies + sm_copies + cv_copies + forwards:
         copy.wait_send()
@@ -390,6 +386,16 @@
     for e in range(1, parts):
         for t in range(HEADS):
             rd_copy(e, t).wait_send()
+
+
+def assemble(dq_tiles, out_tiles, conv, dq_ref, dk_ref, dv_ref):
+    channels = dq_ref.shape[1]
+    turned = dq_tiles[...].astype(F32).reshape(channels, LANES).T
+    dq_ref[...] = turned.astype(BF16)
+    tiles = [out_tiles[h].astype(F32) for h in range(HEADS)]
+    dk_ref[...] = jnp.concatenate([tile[:, :HD] for tile in tiles], axis=1).astype(BF16)
+    total = jnp.concatenate([tile[:, HD:] for tile in tiles], axis=1) + conv[...]
+    dv_ref[...] = total.astype(BF16)
 
 
 def body(queries, keys, values, outputs, grad_out, block_mask, neighbours, conv_weight):
@@ -401,9 +407,13 @@
     vmem = pl.BlockSpec(memory_space=pltpu.VMEM)
     shape = jax.ShapeDtypeStruct((rows, channels), BF16)
     others = HEADS - 1
-    return pl.pallas_call(
+    dq, out, conv = pl.pallas_call(
         functools.partial(kernel, n, early),
-        out_shape=(shape, shape, shape),
+        out_shape=(
+            jax.ShapeDtypeStruct((HEADS, HD, rows), BF16),
+            jax.ShapeDtypeStruct((HEADS, rows, LANES), BF16),
+            jax.ShapeDtypeStruct((rows, channels), F32),
+        ),
         in_specs=[vmem] * 8,
         out_specs=(vmem, vmem, vmem),
         scratch_shapes=[
@@ -451,6 +461,12 @@
             collective_id=0, has_side_effects=True, vmem_limit_bytes=60 * 2**20
         ),
     )(queries, keys, values, outputs, grad_out, block_mask, neighbours.T, conv_weight)
+    return pl.pallas_call(
+        assemble,
+        out_shape=(shape, shape, shape),
+        in_specs=[vmem] * 3,
+        out_specs=(vmem, vmem, vmem),
+    )(dq, out, conv)
 
 
 def solution(mesh):

time: 48.1 us -> 43.6 us (0.906)
  local copies, waits for them, and re-layouts: 3.21 us -> 0 us
  Pallas kernels: 44.1 us -> 42.8 us
    unnamed x7 -> x0, local copies, waits for them, and re-layouts: 3.21 us -> none
    pallas_call x1 -> x2, Pallas kernels: 44.1 us -> 42.8 us  [the longest x1 40.8 us: body(): pl.pallas_call(functools.partial(kernel, n, early), out_shape=(jax.ShapeD...]
where the time goes in v3:
time: 43.6 us; the launch traced here: 43.4 us
  Pallas kernels  42.8 us (98%)
  between operations  0.64 us (1%)
    pallas_call x1, Pallas kernels, body(): pl.pallas_call(functools.partial(kernel, n, early), out_shape=(jax.ShapeD...  40.8 us
    pallas_call x1, Pallas kernels, body(): pl.pallas_call(assemble, out_shape=(shape, shape, shape), in_specs=[vmem]...  1.95 us

profile of v3, /device:TPU:0, one launch (start us, length us, event | category | flops | bytes accessed | tf_op | source)
XLA Modules:
  0.0 43.4 jit_solution(313587237850992003)
XLA Ops:
  0.6 40.8 %shard_map.103 = (bf16[8,64,128]{2,1,0:T(8,128)(2,1)}, bf16[8,128,128]{2,1,0:T(8,128)(2,1)}, f32[128,512]{1,0:T(8,128)}) custom-call(bf16[128,512]{1,0:T(8,128)(2,1)} %q_ref.1, bf16[128,512]{1,0:T(8,128)(2,1)} %k_ref.1, bf16[128,512]{1,0:T(8,128)(2,1)} %v_ref.1, bf16[128,512]{1,0:T(8,128)(2,1)} %o_ref.1, bf16[128,512]{1,0:T(8,128)(2,1)} %g_ref.1, ...), custom_call_target="tpu_custom_call" | custom-call | tf_op jit(solution)/shard_map/pallas_call | solution.py:410
  41.5 2.0 %shard_map.104 = (bf16[128,512]{1,0:T(8,128)(2,1)}, bf16[128,512]{1,0:T(8,128)(2,1)}, bf16[128,512]{1,0:T(8,128)(2,1)}) custom-call(bf16[8,64,128]{2,1,0:T(8,128)(2,1)} %get-tuple-element.6.dq_tiles, bf16[8,128,128]{2,1,0:T(8,128)(2,1)} %get-tuple-element.7.out_tiles, f32[128,512]{1,0:T(8,128)} %get-tuple-element.8.conv), custom_call_target="tpu_custom_call" | custom-call | tf_op jit(solution)/shard_map/pallas_call | solution.py:464
